TPU v7x, 128 devices: a whole 4x4x4 slice. The times are simulated.
128 devices in a mesh: row: 16 (over y, x_hi, core), col: 8 (over x_lo, z).
Axes of the slice: x: 4 (x_hi: 2, x_lo: 2; x = x_hi * 2 + x_lo), y: 4, z: 4, core: 2. Of those that a mesh axis runs over, the one named last changes fastest.
Arguments:
- pair: bfloat16 [448, 448, 128], P('row', 'col'), may hold values from -6 to 6
- cotangent: bfloat16 [448, 448, 128], P('row', 'col'), may hold values from -6 to 6
- w_a_proj: bfloat16 [128, 128], replicated, may hold values from -0.5 to 0.5
- w_a_gate: bfloat16 [128, 128], replicated, may hold values from -0.5 to 0.5
- w_b_proj: bfloat16 [128, 128], replicated, may hold values from -0.5 to 0.5
- w_b_gate: bfloat16 [128, 128], replicated, may hold values from -0.5 to 0.5
- w_gate: bfloat16 [128, 128], replicated, may hold values from -0.5 to 0.5
- w_out: bfloat16 [128, 128], replicated, may hold values from -0.5 to 0.5
- in_gain: float32 [128], replicated, may hold values from 0.5 to 1.5
- in_bias: float32 [128], replicated, may hold values from -1.5 to 1.5
- mid_gain: float32 [128], replicated, may hold values from 0.1 to 1.9
- mid_bias: float32 [128], replicated, may hold values from -1.5 to 1.5
- drop_bits: int32 [448, 128], P('row'), may hold values 0 or 1
- tok_mask: int32 [448], replicated, may hold values from 0 to 1, as said below
Outputs:
- result: bfloat16 [448, 448, 128], P('row', 'col')
- pair_grad: bfloat16 [448, 448, 128], P('row', 'col')
- a_proj_grad: float32 [128, 128], replicated
- a_gate_grad: float32 [128, 128], replicated
- b_proj_grad: float32 [128, 128], replicated
- b_gate_grad: float32 [128, 128], replicated
- gate_grad: float32 [128, 128], replicated
- out_grad: float32 [128, 128], replicated
- in_gain_grad: float32 [128], replicated
- in_bias_grad: float32 [128], replicated
- mid_gain_grad: float32 [128], replicated
- mid_bias_grad: float32 [128], replicated
Inputs may be any that keep to these rules, and one draw needn't show every extreme that they name: `tok_mask`: 1 on the live tokens, which form a prefix of 224 or more tokens, 0 on the rest; at least one token is padding.
All inputs are finite; a program needn't handle non-finite values. No bound on the sum of `drop_bits` on one device may be relied on, other than what follows from the above.
Results may differ from a plain program's by a relative error of at most 0.012.
Values may be sent and summed in bfloat16 or wider, within the bound.
A program may use at most 128 MiB of HBM per device.

v0:
```python
import jax
import jax.numpy as jnp
from jax import lax
from jax.experimental import pallas as pl
from jax.experimental.pallas import tpu as pltpu
from jax.sharding import PartitionSpec as P

LN_EPS = 1e-05
KEEP_RATE = 0.75
ROWS, COLS = 16, 8
DEVICES = ROWS * COLS
TR, TC = 28, 56
TOKENS = 448
WIDE = 256
STEPS = 7
CELLS = WIDE * STEPS
SIDE = 512
PART = 16
HALF = 14
ORDER = 45
OWNERS = DEVICES // 2
BF16 = jnp.bfloat16
F32 = jnp.float32


def dot(left, right):
    return jnp.dot(left, right, preferred_element_type=F32)


def dot_nt(left, right):
    return lax.dot_general(left, right, (((1,), (1,)), ((), ())), preferred_element_type=F32)


def dot_tn(left, right):
    return lax.dot_general(left, right, (((0,), (0,)), ((), ())), preferred_element_type=F32)


def mean0(values):
    return jnp.mean(values, axis=0, keepdims=True)


def swap_halves(first, second):
    low = lax.broadcasted_iota(jnp.int32, first.shape, 1) < 64
    turned_first = pltpu.roll(first, 64, 1)
    turned_second = pltpu.roll(second, 64, 1)
    return jnp.where(low, first, turned_second), jnp.where(low, turned_first, second)


def kernel(
    pair,
    cot,
    w_a_proj,
    w_a_gate,
    w_b_proj,
    w_b_gate,
    w_gate,
    w_out,
    in_gain,
    in_bias,
    mid_gain,
    mid_bias,
    drop,
    tok,
    result,
    pair_grad,
    sums,
    send_ab,
    send_p,
    send_d,
    send_ga,
    send_gb,
    got_ab,
    got_p,
    got_d,
    got_ga,
    got_gb,
    left,
    right,
    turn,
    square,
    flat_ab,
    flat_a,
    flat_b,
    eye,
    w_in_t,
    w_out_t,
    w_all,
    columns,
    drop_wide,
    stack,
    hat,
    scale,
    keep_a,
    slope_a,
    keep_b,
    slope_b,
    pair_t,
    cot_t,
    lift_keep,
    logit_keep,
    d_lifted,
    grad_mixed,
    mid_hat,
    mixed,
    d_all,
    totals,
    sums_flat,
    sums_send,
    sums_got,
    share,
    send_sem,
    recv_sem,
):
    row, col = lax.axis_index("row"), lax.axis_index("col")
    me = row * COLS + col
    barrier = pltpu.get_barrier_semaphore()

    def place(peer):
        return (peer // COLS, lax.rem(peer, COLS))

    def greet(step, carry):
        pl.semaphore_signal(
            barrier,
            inc=1,
            device_id=place(lax.rem(me + step, DEVICES)),
            device_id_type=pl.DeviceIdType.MESH,
        )
        return carry

    lax.fori_loop(1, DEVICES, greet, 0)

    def send(source, target, slot, size=PART):
        mine = pl.ds(pl.multiple_of(me * size, size), size)

        def start(step, carry):
            peer = lax.rem(me + step * ORDER, DEVICES)
            pltpu.make_async_remote_copy(
                src_ref=source.at[pl.ds(pl.multiple_of(peer * size, size), size)],
                dst_ref=target.at[mine],
                send_sem=send_sem.at[slot],
                recv_sem=recv_sem.at[slot],
                device_id=place(peer),
                device_id_type=pl.DeviceIdType.MESH,
            ).start()
            return carry

        lax.fori_loop(1, DEVICES, start, 0)
        target[mine] = source[mine]

    def settle(ref, sem, slot, length):
        some = ref.at[pl.ds(0, length)]
        pltpu.make_async_copy(some, some, sem.at[slot]).wait()

    def arrived(target, slot, size=PART):
        settle(target, recv_sem, slot, (DEVICES - 1) * size)

    def lanes(step):
        return pl.ds(pl.multiple_of(step * WIDE, WIDE), WIDE)

    def each(body):
        def run(step, carry):
            body(step, lanes(step))
            return carry

        lax.fori_loop(0, STEPS, run, 0, unroll=STEPS)

    def scatter(flat, step, values, stride=PART, shift=0):
        flat[pl.ds(2 * step + shift, 128, stride=stride), :] = values[:, :128]
        flat[pl.ds(2 * step + shift + 1, 128, stride=stride), :] = values[:, 128:]

    def gather(flat, step):
        return jnp.concatenate(
            [
                flat[pl.ds(2 * step, 128, stride=PART), :],
                flat[pl.ds(2 * step + 1, 128, stride=PART), :],
            ],
            axis=1,
        )

    def turned(ref, step):
        return jnp.concatenate(
            [dot_nt(eye[...], ref[2 * step]), dot_nt(eye[...], ref[2 * step + 1])], axis=1
        )

    def turn_back(ref, step, values):
        ref[2 * step] = dot_nt(eye[...], values[:, :128]).astype(BF16)
        ref[2 * step + 1] = dot_nt(eye[...], values[:, 128:]).astype(BF16)

    def assemble(blocks, matrix, stride=PART, shift=0):
        def run(index, carry):
            base = pl.multiple_of(index * COLS * stride, COLS * stride)
            top = pl.multiple_of(index * 32, 32)
            for pick in range(4):
                one = blocks[pl.ds(base + 2 * pick * stride + shift, PART)].astype(F32)
                two = blocks[pl.ds(base + (2 * pick + 1) * stride + shift, PART)].astype(F32)
                upper, lower = swap_halves(one, two)
                here = pl.ds(128 * pick, 128)
                matrix[pl.ds(top, PART), here] = upper.astype(BF16)
                matrix[pl.ds(top + PART, PART), here] = lower.astype(BF16)
            return carry

        lax.fori_loop(0, ROWS, run, 0, unroll=ROWS)

    def split(matrix, blocks):
        def run(index, carry):
            base = pl.multiple_of(index * 128, 128)
            top = pl.multiple_of(index * 32, 32)
            for pick in range(4):
                here = pl.ds(128 * pick, 128)
                upper = matrix[pl.ds(top, PART), here]
                lower = matrix[pl.ds(top + PART, PART), here]
                one, two = swap_halves(upper, lower)
                blocks[pl.ds(base + 32 * pick, PART)] = one.astype(BF16)
                blocks[pl.ds(base + 32 * pick + PART, PART)] = two.astype(BF16)
            return carry

        lax.fori_loop(0, ROWS, run, 0, unroll=ROWS)

    eye[...] = (
        lax.broadcasted_iota(jnp.int32, (128, 128), 0)
        == lax.broadcasted_iota(jnp.int32, (128, 128), 1)
    ).astype(BF16)
    for place_of, weight in enumerate((w_a_proj, w_a_gate, w_b_proj, w_b_gate, w_gate)):
        here = slice(128 * place_of, 128 * place_of + 128)
        w_in_t[here] = dot_nt(eye[...], weight[...]).astype(BF16)
        w_all[:, here] = weight[...]
    w_out_t[...] = dot_nt(eye[...], w_out[...]).astype(BF16)
    for place_of, vector in enumerate((in_gain, in_bias, mid_gain, mid_bias)):
        column = jnp.broadcast_to(vector[...], (128, 128)).T
        columns[place_of] = jnp.concatenate([column, column], axis=1)
    stack[256:272] = jnp.ones((16, CELLS), BF16)
    flat_ab[...] = jnp.zeros_like(flat_ab)
    flat_b[...] = jnp.zeros_like(flat_b)
    drop_wide[...] = jnp.zeros_like(drop_wide)
    drop_wide[0:TR] = drop[...].astype(F32)
    live = jnp.sum(tok[...].astype(F32), axis=1, keepdims=True)

    def cell_mask(step):
        lane = lax.broadcasted_iota(jnp.int32, (1, WIDE), 1)
        tile_row = ((lane >> 6) & 1) * HALF + (lane >> 7) + 2 * step
        within = lane & 15
        tile_col = ((lane >> 4) & 3) * HALF + within
        grid_row = (tile_row + row * TR).astype(F32)
        grid_col = (tile_col + col * TC).astype(F32)
        one = jnp.where(grid_row < live, 1.0, 0.0) * jnp.where(grid_col < live, 1.0, 0.0)
        return one * jnp.where(within < HALF, 1.0, 0.0)

    def front(step, here, weights, keep, slope, shift):
        logits = dot(w_in_t[weights], stack[0:128, here])
        squash = jax.nn.sigmoid(logits[128:])
        masked = squash * cell_mask(step)
        values = logits[:128] * masked
        keep[:, here] = masked
        slope[:, here] = values * (1.0 - squash)
        scatter(flat_ab, step, values, 2 * PART, shift)

    def front_a(step, here):
        cells = turned(pair, step)
        pair_t[:, here] = cells
        centered = cells - mean0(cells)
        root = lax.rsqrt(mean0(centered * centered) + LN_EPS)
        rough = centered * root
        hat[:, here] = rough
        scale[:, here] = root
        stack[0:128, here] = (rough * columns[0] + columns[1]).astype(BF16)
        stack[128:256, here] = rough.astype(BF16)
        front(step, here, slice(0, 256), keep_a, slope_a, 0)
        front(step, here, slice(256, 512), keep_b, slope_b, PART)

    each(front_a)
    send_ab[...] = flat_ab[...].astype(BF16)
    pl.semaphore_wait(barrier, DEVICES - 1)
    send(send_ab, got_ab, 0, 2 * PART)

    def prepare(step, here):
        squash = jax.nn.sigmoid(dot(w_in_t[512:640], stack[0:128, here]))
        lane = lax.broadcasted_iota(jnp.int32, (32, WIDE), 1)
        chosen = ((lane >> 6) & 1) * HALF + (lane >> 7) + 2 * step
        pick = (lax.broadcasted_iota(jnp.int32, (32, WIDE), 0) == chosen).astype(BF16)
        bits = dot_tn(drop_wide[...].astype(BF16), pick)
        kept = bits * (1.0 / KEEP_RATE)
        upstream = turned(cot, step)
        cot_t[:, here] = upstream
        lift_keep[:, here] = kept * squash
        pulled = upstream * kept * squash
        logit_keep[:, here] = pulled * (1.0 - squash)
        lifted_back = pulled.astype(BF16)
        d_lifted[:, here] = lifted_back
        grad_mixed[:, here] = dot(w_out[...], lifted_back)

    each(prepare)
    arrived(got_ab, 0, 2 * PART)
    assemble(got_ab, left, 2 * PART)
    assemble(got_ab, right, 2 * PART, PART)
    square[...] = dot_tn(left[...], right[...])
    split(square, send_p)
    send(send_p, got_p, 2)

    arrived(got_p, 2)
    flat_a[...] = got_p[...].astype(F32)

    def tail_back(step, here):
        cells = gather(flat_a, step)
        centered = cells - mean0(cells)
        root = lax.rsqrt(mean0(centered * centered) + LN_EPS)
        rough = centered * root
        mid_hat[:, here] = rough
        pulled = grad_mixed[:, here] * columns[2]
        scatter(flat_b, step, root * (pulled - mean0(pulled) - rough * mean0(pulled * rough)))

    each(tail_back)
    send_d[...] = flat_b[...].astype(BF16)
    send(send_d, got_d, 3)

    totals[...] = jnp.zeros_like(totals)

    def total(which, values):
        totals[which] += values[:, :128] + values[:, 128:]

    def tail_front(step, here):
        rough = mid_hat[:, here]
        blended = (rough * columns[2] + columns[3]).astype(BF16)
        mixed[:, here] = blended
        lifted = dot(w_out_t[...], blended)
        turn_back(result, step, (pair_t[:, here] + lift_keep[:, here] * lifted).astype(BF16))
        logit = (logit_keep[:, here] * lifted).astype(BF16)
        d_all[512:640, here] = logit
        pulled = grad_mixed[:, here]
        total(2, pulled * rough)
        total(3, pulled)

    each(tail_front)
    sums_flat[...] = jnp.zeros_like(sums_flat)

    def put_sums(which, values):
        sums_flat[pl.ds(which, OWNERS, stride=PART), :] = values[:OWNERS]
        sums_flat[pl.ds(which + 6, OWNERS, stride=PART), :] = values[OWNERS:]

    def put_front(first, last):
        outer = dot_nt(stack[...], d_all[128 * first : 128 * last])
        for which in range(first, last):
            here = slice(128 * (which - first), 128 * (which - first) + 128)
            put_sums(which, outer[0:128, here])
            weight = w_all[:, 128 * which : 128 * which + 128].astype(F32)
            totals[0] += outer[128:256, here] * weight
            totals[1] += outer[256:257, here] * weight

    def put_vector(which):
        sums_flat[12 + which : 13 + which] = jnp.sum(totals[which].T, axis=0, keepdims=True)

    put_front(4, 5)
    put_sums(5, dot_nt(mixed[...], d_lifted[...]))
    put_vector(2)
    put_vector(3)

    arrived(got_d, 3)
    assemble(got_d, turn)
    square[...] = dot_nt(right[...], turn[...])
    split(square, send_ga)
    send(send_ga, got_ga, 4)
    square[...] = dot(left[...], turn[...])
    split(square, send_gb)
    send(send_gb, got_gb, 5)

    def front_back(first, flat, keep, slope):
        def run(step, here):
            cells = gather(flat, step)
            d_all[first : first + 128, here] = (cells * keep[:, here]).astype(BF16)
            d_all[first + 128 : first + 256, here] = (cells * slope[:, here]).astype(BF16)

        return run

    arrived(got_ga, 4)
    flat_a[...] = got_ga[...].astype(F32)
    each(front_back(0, flat_a, keep_a, slope_a))
    put_front(0, 2)
    arrived(got_gb, 5)
    flat_b[...] = got_gb[...].astype(F32)
    each(front_back(256, flat_b, keep_b, slope_b))
    put_front(2, 4)
    put_vector(0)
    put_vector(1)
    sums_send[...] = sums_flat[...].astype(BF16)

    core = lax.rem(row, 2)
    chip = (row // 2) * COLS + col
    mine = pl.ds(pl.multiple_of(me * PART, PART), PART)
    owned = pl.ds(pl.multiple_of(chip * PART, PART), PART)

    def start_sum(step, carry):
        owner = lax.rem(chip + step * ORDER, OWNERS)
        pltpu.make_async_remote_copy(
            src_ref=sums_send.at[pl.ds(pl.multiple_of(owner * PART, PART), PART)],
            dst_ref=sums_got.at[mine],
            send_sem=send_sem.at[6],
            recv_sem=recv_sem.at[6],
            device_id=((owner // COLS) * 2, lax.rem(owner, COLS)),
            device_id_type=pl.DeviceIdType.MESH,
        ).start()
        return carry

    lax.fori_loop(1, OWNERS, start_sum, 0)

    @pl.when(core == 1)
    def _():
        start_sum(0, 0)

    def finish(step, here):
        pulled = dot(w_all[...], d_all[:, here]) * columns[0]
        rough = hat[:, here]
        back = scale[:, here] * (pulled - mean0(pulled) - rough * mean0(pulled * rough))
        turn_back(pair_grad, step, (cot_t[:, here] + back).astype(BF16))

    each(finish)

    @pl.when(core == 0)
    def _():
        sums_got[mine] = sums_send[owned]
        arrived(sums_got, 6)
        whole = jnp.sum(sums_got[...].astype(F32).reshape(DEVICES, PART, 128), axis=0)
        share[...] = (whole * (1.0 / TOKENS)).astype(BF16)

        def start_share(step, carry):
            pltpu.make_async_remote_copy(
                src_ref=share,
                dst_ref=sums.at[owned],
                send_sem=send_sem.at[7],
                recv_sem=recv_sem.at[7],
                device_id=place(lax.rem(me + step * ORDER, DEVICES)),
                device_id_type=pl.DeviceIdType.MESH,
            ).start()
            return carry

        lax.fori_loop(1, DEVICES, start_share, 0)
        sums[owned] = share[...]
        settle(sums, recv_sem, 7, (OWNERS - 1) * PART)
        settle(sums_got, send_sem, 7, (DEVICES - 1) * PART)
        settle(sums_send, send_sem, 6, (OWNERS - 1) * PART)

    @pl.when(core == 1)
    def _():
        settle(sums, recv_sem, 7, OWNERS * PART)
        settle(sums_send, send_sem, 6, OWNERS * PART)

    settle(send_ab, send_sem, 0, (DEVICES - 1) * 2 * PART)
    for slot, source in ((2, send_p), (3, send_d), (4, send_ga), (5, send_gb)):
        settle(source, send_sem, slot, (DEVICES - 1) * PART)


def spread(tile):
    padded = jnp.pad(tile.reshape(2, HALF, 4, HALF, 128), ((0, 0),) * 3 + ((0, 2), (0, 0)))
    return padded.transpose(1, 0, 2, 3, 4).reshape(HALF, 128, 128)


def gathered(cells):
    tile = cells.reshape(HALF, 2, 4, 16, 128)[:, :, :, :HALF].transpose(1, 0, 2, 3, 4)
    return tile.reshape(TR, TC, 128)


def body(pair, cotangent, *rest):
    weights, vectors, drop_bits, tok_mask = rest[:6], rest[6:10], rest[10], rest[11]
    vmem = pltpu.VMEM
    block, double = vmem((DEVICES * PART, 128), BF16), vmem((DEVICES * 2 * PART, 128), BF16)
    blocks = [double] + [block] * 4 + [double] + [block] * 4
    squares = [vmem((SIDE, SIDE), BF16)] * 3 + [vmem((SIDE, SIDE), F32)]
    flats = [vmem((DEVICES * 2 * PART, 128), F32)] + [vmem((DEVICES * PART, 128), F32)] * 2
    half, full = vmem((128, CELLS), BF16), vmem((128, CELLS), F32)
    scratch = blocks + squares + flats
    scratch += [vmem((128, 128), BF16), vmem((640, 128), BF16), vmem((128, 128), BF16)]
    scratch += [vmem((128, 640), BF16), vmem((4, 128, WIDE), F32), vmem((32, 128), F32)]
    scratch += [vmem((272, CELLS), BF16), full, vmem((1, CELLS), F32)] + [full] * 8
    scratch += [half, full, full, half, vmem((640, CELLS), BF16)]
    scratch += [vmem((4, 128, 128), F32), vmem((OWNERS * PART, 128), F32)]
    scratch += [vmem((OWNERS * PART, 128), BF16), block, vmem((PART, 128), BF16)]
    scratch += [pltpu.SemaphoreType.DMA((8,)), pltpu.SemaphoreType.DMA((8,))]
    result, pair_grad, sums = pl.pallas_call(
        kernel,
        out_shape=(
            jax.ShapeDtypeStruct((HALF, 128, 128), BF16),
            jax.ShapeDtypeStruct((HALF, 128, 128), BF16),
            jax.ShapeDtypeStruct((OWNERS * PART, 128), BF16),
        ),
        in_specs=[pl.BlockSpec(memory_space=vmem)] * 14,
        out_specs=[pl.BlockSpec(memory_space=vmem)] * 3,
        scratch_shapes=scratch,
        compiler_params=pltpu.CompilerParams(
            collective_id=0, has_side_effects=True, vmem_limit_bytes=50 * 2**20
        ),
    )(
        spread(pair),
        spread(cotangent),
        *weights,
        *(vector.reshape(1, 128) for vector in vectors),
        drop_bits,
        tok_mask.reshape(1, TOKENS),
    )
    sums = sums.reshape(OWNERS, PART, 128).astype(F32)
    return (
        (gathered(result), gathered(pair_grad))
        + tuple(
            jnp.concatenate([sums[:, which], sums[:, which + 6]], axis=0) for which in range(6)
        )
        + tuple(sums[0, 12 + which] for which in range(4))
    )


def solution(mesh):
    tiles = P("row", "col", None)
    return jax.shard_map(
        body,
        mesh=mesh,
        in_specs=(tiles, tiles) + (P(),) * 10 + (P("row", None), P()),
        out_specs=(tiles, tiles) + (P(),) * 10,
        check_vma=False,
    )
```

profile of v0, /device:TPU:1, one launch (start us, length us, event | category | flops | bytes accessed | tf_op | source)
XLA Modules:
  0.0 91.3 jit_solution(8993472620350514530)
XLA Ops:
  0.6 1.1 %reshape.66 = bf16[2,14,4,14,128]{4,3,2,1,0:T(8,128)(2,1)S(1)} reshape(bf16[28,56,128]{2,1,0:T(8,128)(2,1)} %param.14) | data formatting | bytes 802816 | tf_op jit(solution)/shard_map/reshape | solution.py:451
  1.8 0.1 pad_bitcast_fusion.1
  1.9 0.0 copy-start.12
  1.9 1.0 %copy-done.12 = bf16[28,56,128]{2,1,0:T(8,128)(2,1)S(1)} copy-done((bf16[28,56,128]{2,1,0:T(8,128)(2,1)S(1)}, bf16[28,56,128]{2,1,0:T(8,128)(2,1)}, u32[]{:S(2)}) %copy-start.12) | copy-done | bytes 401432
  2.9 0.1 reshape.68
  3.0 0.1 pad_bitcast_fusion
  3.1 0.0 copy-start
  3.1 0.0 copy-start.1
  3.1 0.0 copy-start.2
  3.1 0.0 copy-start.3
  3.1 0.0 copy-start.4
  3.2 0.0 copy-start.5
  3.2 0.0 copy-start.6
  3.2 0.0 copy-start.7
  3.2 0.0 copy-start.11
  3.2 0.0 copy-start.8
  3.3 0.0 copy-start.9
  3.3 0.0 copy-start.10
  3.3 0.6 copy-done
  3.9 0.0 copy-done.1
  3.9 0.0 copy-done.2
  3.9 0.0 copy-done.3
  3.9 0.0 copy-done.4
  3.9 0.0 copy-done.5
  4.0 82.7 %shard_map.229 = (bf16[14,128,128]{2,1,0:T(8,128)(2,1)S(1)}, bf16[14,128,128]{2,1,0:T(8,128)(2,1)S(1)}, bf16[1024,128]{1,0:T(8,128)(2,1)S(1)}) custom-call(bf16[14,128,128]{2,1,0:T(8,128)(2,1)S(1)} %bitcast.63, bf16[14,128,128]{2,1,0:T(8,128)(2,1)S(1)} %bitcast.64, bf16[128,128]{1,0:T(8,128)(2,1)S(1)} %copy-done, bf16[128,128]{1,0:T(8,128)(2,1)S(1)} %copy-done.1, ...), custom_call_target="tpu_custom_call" | custom-call | tf_op jit(solution)/shard_map/pallas_call | solution.py:476
  86.7 0.9 reshape.76
  87.6 0.9 reshape.78
  88.5 0.3 fusion
  88.8 0.7 pad_maximum_fusion.4
  89.5 0.7 pad_maximum_fusion.2
  90.1 0.7 pad_maximum_fusion
  90.8 0.5 slice_bitcast_fusion
  (11 shorter events, 0.2 us)
Async XLA Ops:
  1.9 1.0 %copy-start.12 = (bf16[28,56,128]{2,1,0:T(8,128)(2,1)S(1)}, bf16[28,56,128]{2,1,0:T(8,128)(2,1)}, u32[]{:S(2)}) copy-start(bf16[28,56,128]{2,1,0:T(8,128)(2,1)} %param.15) | copy-start | bytes 1204228
  3.1 0.8 copy-start
  3.1 0.8 copy-start.1
  3.1 0.8 copy-start.2
  3.1 0.8 copy-start.3
  3.1 0.8 copy-start.4
  3.2 0.8 copy-start.5
  3.2 0.8 copy-start.6
  3.2 0.8 copy-start.7
  3.2 0.8 copy-start.11
  3.2 0.7 copy-start.8
  3.3 0.7 copy-start.9
  3.3 0.7 copy-start.10
where the time goes:
time: 91.6 us; the launch traced here: 91.3 us
  Pallas kernels  82.7 us (90%)
  local copies, waits for them, and re-layouts  5.81 us (6%)
  other arithmetic  2.01 us (2%)
    pallas_call x1, Pallas kernels, body(): pl.pallas_call(kernel, out_shape=(jax.ShapeDtypeStruct((HALF, 128, 128),...  82.7 us
    concatenate x3, other arithmetic, body(): jnp.concatenate([sums[:, which], sums[:, which + 6]], axis=0)  1.97 us

commit v1 on v0

--- a/solution.py
+++ b/solution.py
@@ -17,10 +17,27 @@
 SIDE = 512
 PART = 16
 HALF = 14
-ORDER = 45
 OWNERS = DEVICES // 2
 BF16 = jnp.bfloat16
 F32 = jnp.float32
+
+
+def partners(cores):
+    offsets = [
+        (x, y, z, core)
+        for x in range(4)
+        for y in range(4)
+        for z in range(4)
+        for core in range(cores)
+        if x or y or z or core
+    ]
+
+    def rank(offset):
+        far = sum(min(step, 4 - step) for step in offset[:3])
+        x, y, z, core = offset
+        return -far, (29 * x + 13 * y + 7 * z + 17 * core) % 31, offset
+
+    return sorted(offsets, key=rank)
 
 
 def dot(left, right):
@@ -46,23 +63,19 @@
     return jnp.where(low, first, turned_second), jnp.where(low, turned_first, second)
 
 
-def kernel(
-    pair,
-    cot,
-    w_a_proj,
-    w_a_gate,
-    w_b_proj,
-    w_b_gate,
-    w_gate,
-    w_out,
-    in_gain,
-    in_bias,
-    mid_gain,
-    mid_bias,
-    drop,
-    tok,
-    result,
-    pair_grad,
+def kernel(*refs):
+    inputs, refs = refs[:14], refs[14:]
+    outputs, refs = refs[:3], refs[3:]
+    run_kernel(inputs, outputs, refs[:8], *refs[8:])
+
+
+def run_kernel(
+    inputs,
+    outputs,
+    local,
+    result_cells,
+    grad_cells,
+    pick_cells,
     sums,
     send_ab,
     send_p,
@@ -110,7 +123,17 @@
     share,
     send_sem,
     recv_sem,
+    local_sem,
 ):
+    in_gain, in_bias, mid_gain, mid_bias, drop, tok = inputs[8:]
+    result, pair_grad, all_sums = outputs
+    pair, cot, w_a_proj, w_a_gate, w_b_proj, w_b_gate, w_gate, w_out = local
+    fetches = [
+        pltpu.make_async_copy(inputs[which], local[which], local_sem.at[which])
+        for which in range(8)
+    ]
+    for fetch in fetches:
+        fetch.start()
     row, col = lax.axis_index("row"), lax.axis_index("col")
     me = row * COLS + col
     barrier = pltpu.get_barrier_semaphore()
@@ -129,11 +152,22 @@
 
     lax.fori_loop(1, DEVICES, greet, 0)
 
+    core = lax.rem(row, 2)
+    at_x, at_y, at_z = lax.rem(row // 2, 2) * 2 + col // 4, row // 4, lax.rem(col, 4)
+    steps_x = [lax.rem(at_x + step, 4) for step in range(4)]
+    part_x = [(step // 2) * 16 + lax.rem(step, 2) * 4 for step in steps_x]
+    part_y = [lax.rem(at_y + step, 4) * 32 for step in range(4)]
+    part_z = [lax.rem(at_z + step, 4) for step in range(4)]
+    part_core = [lax.rem(core + step, 2) * 8 for step in range(2)]
+
+    def device_at(x, y, z, other_core):
+        return part_x[x] + part_y[y] + part_z[z] + part_core[other_core]
+
     def send(source, target, slot, size=PART):
         mine = pl.ds(pl.multiple_of(me * size, size), size)
 
-        def start(step, carry):
-            peer = lax.rem(me + step * ORDER, DEVICES)
+        for offset in partners(2):
+            peer = device_at(*offset)
             pltpu.make_async_remote_copy(
                 src_ref=source.at[pl.ds(pl.multiple_of(peer * size, size), size)],
                 dst_ref=target.at[mine],
@@ -142,9 +176,6 @@
                 device_id=place(peer),
                 device_id_type=pl.DeviceIdType.MESH,
             ).start()
-            return carry
-
-        lax.fori_loop(1, DEVICES, start, 0)
         target[mine] = source[mine]
 
     def settle(ref, sem, slot, length):
@@ -177,14 +208,25 @@
             axis=1,
         )
 
+    def tile_rows(step, part):
+        first = pl.multiple_of((2 * step + part) * TC, 8)
+        second = pl.multiple_of((2 * step + part + HALF) * TC, 8)
+        return pl.ds(first, TC), pl.ds(second, TC)
+
     def turned(ref, step):
-        return jnp.concatenate(
-            [dot_nt(eye[...], ref[2 * step]), dot_nt(eye[...], ref[2 * step + 1])], axis=1
-        )
+        parts = []
+        for part in range(2):
+            first, second = tile_rows(step, part)
+            cells = jnp.concatenate([ref[first], ref[second]], axis=0).astype(BF16)
+            parts.append(dot_tn(cells, pick_cells[...]))
+        return jnp.concatenate(parts, axis=1)
 
     def turn_back(ref, step, values):
-        ref[2 * step] = dot_nt(eye[...], values[:, :128]).astype(BF16)
-        ref[2 * step + 1] = dot_nt(eye[...], values[:, 128:]).astype(BF16)
+        for part in range(2):
+            first, second = tile_rows(step, part)
+            cells = dot_nt(pick_cells[...], values[:, 128 * part : 128 * part + 128])
+            ref[first] = cells[:TC]
+            ref[second] = cells[TC:]
 
     def assemble(blocks, matrix, stride=PART, shift=0):
         def run(index, carry):
@@ -220,6 +262,13 @@
         lax.broadcasted_iota(jnp.int32, (128, 128), 0)
         == lax.broadcasted_iota(jnp.int32, (128, 128), 1)
     ).astype(BF16)
+    lane = lax.broadcasted_iota(jnp.int32, (2 * TC, 128), 1)
+    wanted = (lane >> 6) * TC + ((lane >> 4) & 3) * HALF + (lane & 15)
+    chosen_cell = lax.broadcasted_iota(jnp.int32, (2 * TC, 128), 0) == wanted
+    chosen_cell = jnp.where(chosen_cell, 1.0, 0.0) * jnp.where((lane & 15) < HALF, 1.0, 0.0)
+    pick_cells[...] = chosen_cell.astype(BF16)
+    for fetch in fetches:
+        fetch.wait()
     for place_of, weight in enumerate((w_a_proj, w_a_gate, w_b_proj, w_b_gate, w_gate)):
         here = slice(128 * place_of, 128 * place_of + 128)
         w_in_t[here] = dot_nt(eye[...], weight[...]).astype(BF16)
@@ -255,7 +304,7 @@
         scatter(flat_ab, step, values, 2 * PART, shift)
 
     def front_a(step, here):
-        cells = turned(pair, step)
+        cells = turned(result_cells, step)
         pair_t[:, here] = cells
         centered = cells - mean0(cells)
         root = lax.rsqrt(mean0(centered * centered) + LN_EPS)
@@ -267,6 +316,7 @@
         front(step, here, slice(0, 256), keep_a, slope_a, 0)
         front(step, here, slice(256, 512), keep_b, slope_b, PART)
 
+    result_cells[...] = pair[...].astype(F32)
     each(front_a)
     send_ab[...] = flat_ab[...].astype(BF16)
     pl.semaphore_wait(barrier, DEVICES - 1)
@@ -279,7 +329,7 @@
         pick = (lax.broadcasted_iota(jnp.int32, (32, WIDE), 0) == chosen).astype(BF16)
         bits = dot_tn(drop_wide[...].astype(BF16), pick)
         kept = bits * (1.0 / KEEP_RATE)
-        upstream = turned(cot, step)
+        upstream = turned(grad_cells, step)
         cot_t[:, here] = upstream
         lift_keep[:, here] = kept * squash
         pulled = upstream * kept * squash
@@ -288,6 +338,7 @@
         d_lifted[:, here] = lifted_back
         grad_mixed[:, here] = dot(w_out[...], lifted_back)
 
+    grad_cells[...] = cot[...].astype(F32)
     each(prepare)
     arrived(got_ab, 0, 2 * PART)
     assemble(got_ab, left, 2 * PART)
@@ -322,7 +373,7 @@
         blended = (rough * columns[2] + columns[3]).astype(BF16)
         mixed[:, here] = blended
         lifted = dot(w_out_t[...], blended)
-        turn_back(result, step, (pair_t[:, here] + lift_keep[:, here] * lifted).astype(BF16))
+        turn_back(result_cells, step, (pair_t[:, here] + lift_keep[:, here] * lifted).astype(BF16))
         logit = (logit_keep[:, here] * lifted).astype(BF16)
         d_all[512:640, here] = logit
         pulled = grad_mixed[:, here]
@@ -330,6 +381,7 @@
         total(3, pulled)
 
     each(tail_front)
+    result[...] = result_cells[...].astype(BF16)
     sums_flat[...] = jnp.zeros_like(sums_flat)
 
     def put_sums(which, values):
@@ -382,36 +434,37 @@
     put_vector(1)
     sums_send[...] = sums_flat[...].astype(BF16)
 
-    core = lax.rem(row, 2)
     chip = (row // 2) * COLS + col
     mine = pl.ds(pl.multiple_of(me * PART, PART), PART)
     owned = pl.ds(pl.multiple_of(chip * PART, PART), PART)
 
-    def start_sum(step, carry):
-        owner = lax.rem(chip + step * ORDER, OWNERS)
+    def start_sum(x, y, z):
+        home = part_x[x] + part_y[y] + part_z[z]
+        owner = (home // 16) * COLS + lax.rem(home, COLS)
         pltpu.make_async_remote_copy(
             src_ref=sums_send.at[pl.ds(pl.multiple_of(owner * PART, PART), PART)],
             dst_ref=sums_got.at[mine],
             send_sem=send_sem.at[6],
             recv_sem=recv_sem.at[6],
-            device_id=((owner // COLS) * 2, lax.rem(owner, COLS)),
+            device_id=place(home),
             device_id_type=pl.DeviceIdType.MESH,
         ).start()
-        return carry
-
-    lax.fori_loop(1, OWNERS, start_sum, 0)
+
+    for x, y, z, _ in partners(1):
+        start_sum(x, y, z)
 
     @pl.when(core == 1)
     def _():
-        start_sum(0, 0)
+        start_sum(0, 0, 0)
 
     def finish(step, here):
         pulled = dot(w_all[...], d_all[:, here]) * columns[0]
         rough = hat[:, here]
         back = scale[:, here] * (pulled - mean0(pulled) - rough * mean0(pulled * rough))
-        turn_back(pair_grad, step, (cot_t[:, here] + back).astype(BF16))
+        turn_back(grad_cells, step, (cot_t[:, here] + back).astype(BF16))
 
     each(finish)
+    pair_grad[...] = grad_cells[...].astype(BF16)
 
     @pl.when(core == 0)
     def _():
@@ -420,18 +473,16 @@
         whole = jnp.sum(sums_got[...].astype(F32).reshape(DEVICES, PART, 128), axis=0)
         share[...] = (whole * (1.0 / TOKENS)).astype(BF16)
 
-        def start_share(step, carry):
+        for offset in partners(2):
             pltpu.make_async_remote_copy(
                 src_ref=share,
                 dst_ref=sums.at[owned],
                 send_sem=send_sem.at[7],
                 recv_sem=recv_sem.at[7],
-                device_id=place(lax.rem(me + step * ORDER, DEVICES)),
+                device_id=place(device_at(*offset)),
                 device_id_type=pl.DeviceIdType.MESH,
             ).start()
-            return carry
-
-        lax.fori_loop(1, DEVICES, start_share, 0)
+
         sums[owned] = share[...]
         settle(sums, recv_sem, 7, (OWNERS - 1) * PART)
         settle(sums_got, send_sem, 7, (DEVICES - 1) * PART)
@@ -442,19 +493,20 @@
         settle(sums, recv_sem, 7, OWNERS * PART)
         settle(sums_send, send_sem, 6, OWNERS * PART)
 
+    all_sums[...] = sums[...].astype(F32)
     settle(send_ab, send_sem, 0, (DEVICES - 1) * 2 * PART)
     for slot, source in ((2, send_p), (3, send_d), (4, send_ga), (5, send_gb)):
         settle(source, send_sem, slot, (DEVICES - 1) * PART)
 
 
-def spread(tile):
-    padded = jnp.pad(tile.reshape(2, HALF, 4, HALF, 128), ((0, 0),) * 3 + ((0, 2), (0, 0)))
-    return padded.transpose(1, 0, 2, 3, 4).reshape(HALF, 128, 128)
-
-
-def gathered(cells):
-    tile = cells.reshape(HALF, 2, 4, 16, 128)[:, :, :, :HALF].transpose(1, 0, 2, 3, 4)
-    return tile.reshape(TR, TC, 128)
+def hand_out(result, pair_grad, sums, *outputs):
+    outputs[0][...] = result[...]
+    outputs[1][...] = pair_grad[...]
+    for which in range(6):
+        outputs[2 + which][0:OWNERS] = sums[pl.ds(which, OWNERS, stride=PART), :]
+        outputs[2 + which][OWNERS:] = sums[pl.ds(which + 6, OWNERS, stride=PART), :]
+    for which in range(4):
+        outputs[8 + which][...] = sums[12 + which : 13 + which]
 
 
 def body(pair, cotangent, *rest):
@@ -465,43 +517,49 @@
     squares = [vmem((SIDE, SIDE), BF16)] * 3 + [vmem((SIDE, SIDE), F32)]
     flats = [vmem((DEVICES * 2 * PART, 128), F32)] + [vmem((DEVICES * PART, 128), F32)] * 2
     half, full = vmem((128, CELLS), BF16), vmem((128, CELLS), F32)
-    scratch = blocks + squares + flats
+    square, tile = vmem((128, 128), BF16), (TR * TC, 128)
+    scratch = [vmem(tile, BF16)] * 2 + [square] * 6 + [vmem(tile, F32)] * 2
+    scratch += [vmem((2 * TC, 128), BF16), vmem((OWNERS * PART, 128), BF16)]
+    scratch += blocks + squares + flats
     scratch += [vmem((128, 128), BF16), vmem((640, 128), BF16), vmem((128, 128), BF16)]
     scratch += [vmem((128, 640), BF16), vmem((4, 128, WIDE), F32), vmem((32, 128), F32)]
     scratch += [vmem((272, CELLS), BF16), full, vmem((1, CELLS), F32)] + [full] * 8
     scratch += [half, full, full, half, vmem((640, CELLS), BF16)]
     scratch += [vmem((4, 128, 128), F32), vmem((OWNERS * PART, 128), F32)]
     scratch += [vmem((OWNERS * PART, 128), BF16), block, vmem((PART, 128), BF16)]
-    scratch += [pltpu.SemaphoreType.DMA((8,)), pltpu.SemaphoreType.DMA((8,))]
-    result, pair_grad, sums = pl.pallas_call(
+    scratch += [pltpu.SemaphoreType.DMA((8,))] * 3
+    done = pl.pallas_call(
         kernel,
-        out_shape=(
-            jax.ShapeDtypeStruct((HALF, 128, 128), BF16),
-            jax.ShapeDtypeStruct((HALF, 128, 128), BF16),
-            jax.ShapeDtypeStruct((OWNERS * PART, 128), BF16),
-        ),
-        in_specs=[pl.BlockSpec(memory_space=vmem)] * 14,
+        out_shape=[
+            jax.ShapeDtypeStruct(tile, BF16),
+            jax.ShapeDtypeStruct(tile, BF16),
+            jax.ShapeDtypeStruct((OWNERS * PART, 128), F32),
+        ],
+        in_specs=[pl.BlockSpec(memory_space=pl.ANY)] * 8 + [pl.BlockSpec(memory_space=vmem)] * 6,
         out_specs=[pl.BlockSpec(memory_space=vmem)] * 3,
         scratch_shapes=scratch,
         compiler_params=pltpu.CompilerParams(
-            collective_id=0, has_side_effects=True, vmem_limit_bytes=50 * 2**20
+            collective_id=0, has_side_effects=True, vmem_limit_bytes=60 * 2**20
         ),
     )(
-        spread(pair),
-        spread(cotangent),
+        pair.reshape(tile),
+        cotangent.reshape(tile),
         *weights,
         *(vector.reshape(1, 128) for vector in vectors),
         drop_bits,
         tok_mask.reshape(1, TOKENS),
     )
-    sums = sums.reshape(OWNERS, PART, 128).astype(F32)
-    return (
-        (gathered(result), gathered(pair_grad))
-        + tuple(
-            jnp.concatenate([sums[:, which], sums[:, which + 6]], axis=0) for which in range(6)
-        )
-        + tuple(sums[0, 12 + which] for which in range(4))
-    )
+    outs = pl.pallas_call(
+        hand_out,
+        out_shape=[jax.ShapeDtypeStruct(tile, BF16)] * 2
+        + [jax.ShapeDtypeStruct((128, 128), F32)] * 6
+        + [jax.ShapeDtypeStruct((1, 128), F32)] * 4,
+        in_specs=[pl.BlockSpec(memory_space=vmem)] * 3,
+        out_specs=[pl.BlockSpec(memory_space=vmem)] * 12,
+        compiler_params=pltpu.CompilerParams(vmem_limit_bytes=60 * 2**20),
+    )(*done)
+    result, pair_grad = outs[0].reshape(TR, TC, 128), outs[1].reshape(TR, TC, 128)
+    return (result, pair_grad) + tuple(outs[2:8]) + tuple(out.reshape(128) for out in outs[8:])
 
 
 def solution(mesh):

time: 91.6 us -> 82.5 us (0.901)
  local copies, waits for them, and re-layouts: 5.81 us -> 0 us
  other arithmetic: 2.01 us -> 0 us
  Pallas kernels: 82.7 us -> 81.5 us
    reshape x4 -> x0, local copies, waits for them, and re-layouts: 2.97 us -> none  [the longest x2 1.74 us: gathered(): return tile.reshape(TR, TC, 128)]
    concatenate x3 -> x0, other arithmetic: 1.97 us -> none  [body(): jnp.concatenate([sums[:, which], sums[:, which + 6]], axis=0)]
    unnamed x26 -> x0, local copies, waits for them, and re-layouts: 1.68 us -> none
    pallas_call x1 -> x2, Pallas kernels: 82.7 us -> 81.5 us  [the longest x1 79.2 us: body(): pl.pallas_call(kernel, out_shape=[jax.ShapeDtypeStruct(tile, BF16), jax.S...]
where the time goes in v1:
time: 82.5 us; the launch traced here: 82.3 us
  Pallas kernels  81.5 us (99%)
    pallas_call x1, Pallas kernels, body(): pl.pallas_call(kernel, out_shape=[jax.ShapeDtypeStruct(tile, BF16), jax.S...  79.2 us
    pallas_call x1, Pallas kernels, body(): pl.pallas_call(hand_out, out_shape=[jax.ShapeDtypeStruct(tile, BF16)] * 2...  2.34 us

profile of v1, /device:TPU:1, one launch (start us, length us, event | category | flops | bytes accessed | tf_op | source)
XLA Modules:
  0.0 82.3 jit_solution(8502764114184304901)
XLA Ops:
  0.6 79.2 %shard_map.229 = (bf16[1568,128]{1,0:T(8,128)(2,1)}, bf16[1568,128]{1,0:T(8,128)(2,1)}, f32[1024,128]{1,0:T(8,128)}) custom-call(bf16[1568,128]{1,0:T(8,128)(2,1)} %bitcast.13, bf16[1568,128]{1,0:T(8,128)(2,1)} %bitcast.14, bf16[128,128]{1,0:T(8,128)(2,1)} %refs_2_.1, bf16[128,128]{1,0:T(8,128)(2,1)} %refs_3_.1, bf16[128,128]{1,0:T(8,128)(2,1)} %refs_4_.1, ...), custom_call_target="tpu_custom_call" | custom-call | tf_op jit(solution)/shard_map/pallas_call | solution.py:531
  79.8 2.3 %shard_map.230 = (bf16[1568,128]{1,0:T(8,128)(2,1)}, bf16[1568,128]{1,0:T(8,128)(2,1)}, f32[128,128]{1,0:T(8,128)}, f32[128,128]{1,0:T(8,128)}, f32[128,128]{1,0...) custom-call(bf16[1568,128]{1,0:T(8,128)(2,1)} %get-tuple-element.27., ...), custom_call_target="tpu_custom_call" | custom-call | tf_op jit(solution)/shard_map/pallas_call | solution.py:552

commit v2 on v1

--- a/solution.py
+++ b/solution.py
@@ -66,7 +66,7 @@
 def kernel(*refs):
     inputs, refs = refs[:14], refs[14:]
     outputs, refs = refs[:3], refs[3:]
-    run_kernel(inputs, outputs, refs[:8], *refs[8:])
+    run_kernel(inputs, outputs, refs[:14], *refs[14:])
 
 
 def run_kernel(
@@ -77,12 +77,14 @@
     grad_cells,
     pick_cells,
     sums,
-    send_ab,
+    send_a,
+    send_b,
     send_p,
     send_d,
     send_ga,
     send_gb,
-    got_ab,
+    got_a,
+    got_b,
     got_p,
     got_d,
     got_ga,
@@ -91,7 +93,6 @@
     right,
     turn,
     square,
-    flat_ab,
     flat_a,
     flat_b,
     eye,
@@ -125,12 +126,12 @@
     recv_sem,
     local_sem,
 ):
-    in_gain, in_bias, mid_gain, mid_bias, drop, tok = inputs[8:]
     result, pair_grad, all_sums = outputs
-    pair, cot, w_a_proj, w_a_gate, w_b_proj, w_b_gate, w_gate, w_out = local
+    pair, cot, w_a_proj, w_a_gate, w_b_proj, w_b_gate, w_gate, w_out = local[:8]
+    in_gain, in_bias, mid_gain, mid_bias, drop, tok = local[8:]
     fetches = [
         pltpu.make_async_copy(inputs[which], local[which], local_sem.at[which])
-        for which in range(8)
+        for which in range(14)
     ]
     for fetch in fetches:
         fetch.start()
@@ -258,6 +259,9 @@
 
         lax.fori_loop(0, ROWS, run, 0, unroll=ROWS)
 
+    flat_a[...] = jnp.zeros_like(flat_a)
+    flat_b[...] = jnp.zeros_like(flat_b)
+    stack[256:272] = jnp.ones((16, CELLS), BF16)
     eye[...] = (
         lax.broadcasted_iota(jnp.int32, (128, 128), 0)
         == lax.broadcasted_iota(jnp.int32, (128, 128), 1)
@@ -277,9 +281,6 @@
     for place_of, vector in enumerate((in_gain, in_bias, mid_gain, mid_bias)):
         column = jnp.broadcast_to(vector[...], (128, 128)).T
         columns[place_of] = jnp.concatenate([column, column], axis=1)
-    stack[256:272] = jnp.ones((16, CELLS), BF16)
-    flat_ab[...] = jnp.zeros_like(flat_ab)
-    flat_b[...] = jnp.zeros_like(flat_b)
     drop_wide[...] = jnp.zeros_like(drop_wide)
     drop_wide[0:TR] = drop[...].astype(F32)
     live = jnp.sum(tok[...].astype(F32), axis=1, keepdims=True)
@@ -294,14 +295,14 @@
         one = jnp.where(grid_row < live, 1.0, 0.0) * jnp.where(grid_col < live, 1.0, 0.0)
         return one * jnp.where(within < HALF, 1.0, 0.0)
 
-    def front(step, here, weights, keep, slope, shift):
+    def front(step, here, weights, keep, slope, flat):
         logits = dot(w_in_t[weights], stack[0:128, here])
         squash = jax.nn.sigmoid(logits[128:])
         masked = squash * cell_mask(step)
         values = logits[:128] * masked
         keep[:, here] = masked
         slope[:, here] = values * (1.0 - squash)
-        scatter(flat_ab, step, values, 2 * PART, shift)
+        scatter(flat, step, values)
 
     def front_a(step, here):
         cells = turned(result_cells, step)
@@ -313,14 +314,16 @@
         scale[:, here] = root
         stack[0:128, here] = (rough * columns[0] + columns[1]).astype(BF16)
         stack[128:256, here] = rough.astype(BF16)
-        front(step, here, slice(0, 256), keep_a, slope_a, 0)
-        front(step, here, slice(256, 512), keep_b, slope_b, PART)
+        front(step, here, slice(0, 256), keep_a, slope_a, flat_a)
 
     result_cells[...] = pair[...].astype(F32)
     each(front_a)
-    send_ab[...] = flat_ab[...].astype(BF16)
+    send_a[...] = flat_a[...].astype(BF16)
     pl.semaphore_wait(barrier, DEVICES - 1)
-    send(send_ab, got_ab, 0, 2 * PART)
+    send(send_a, got_a, 0)
+    each(lambda step, here: front(step, here, slice(256, 512), keep_b, slope_b, flat_b))
+    send_b[...] = flat_b[...].astype(BF16)
+    send(send_b, got_b, 1)
 
     def prepare(step, here):
         squash = jax.nn.sigmoid(dot(w_in_t[512:640], stack[0:128, here]))
@@ -340,9 +343,10 @@
 
     grad_cells[...] = cot[...].astype(F32)
     each(prepare)
-    arrived(got_ab, 0, 2 * PART)
-    assemble(got_ab, left, 2 * PART)
-    assemble(got_ab, right, 2 * PART, PART)
+    arrived(got_a, 0)
+    assemble(got_a, left)
+    arrived(got_b, 1)
+    assemble(got_b, right)
     square[...] = dot_tn(left[...], right[...])
     split(square, send_p)
     send(send_p, got_p, 2)
@@ -381,7 +385,9 @@
         total(3, pulled)
 
     each(tail_front)
-    result[...] = result_cells[...].astype(BF16)
+    pair[...] = result_cells[...].astype(BF16)
+    hand_result = pltpu.make_async_copy(pair, result, local_sem.at[14])
+    hand_result.start()
     sums_flat[...] = jnp.zeros_like(sums_flat)
 
     def put_sums(which, values):
@@ -464,7 +470,9 @@
         turn_back(grad_cells, step, (cot_t[:, here] + back).astype(BF16))
 
     each(finish)
-    pair_grad[...] = grad_cells[...].astype(BF16)
+    cot[...] = grad_cells[...].astype(BF16)
+    hand_grad = pltpu.make_async_copy(cot, pair_grad, local_sem.at[15])
+    hand_grad.start()
 
     @pl.when(core == 0)
     def _():
@@ -493,32 +501,57 @@
         settle(sums, recv_sem, 7, OWNERS * PART)
         settle(sums_send, send_sem, 6, OWNERS * PART)
 
-    all_sums[...] = sums[...].astype(F32)
-    settle(send_ab, send_sem, 0, (DEVICES - 1) * 2 * PART)
-    for slot, source in ((2, send_p), (3, send_d), (4, send_ga), (5, send_gb)):
+    hand_sums = pltpu.make_async_copy(sums, all_sums, local_sem.at[16])
+    hand_sums.start()
+    for slot, source in enumerate((send_a, send_b, send_p, send_d, send_ga, send_gb)):
         settle(source, send_sem, slot, (DEVICES - 1) * PART)
-
-
-def hand_out(result, pair_grad, sums, *outputs):
-    outputs[0][...] = result[...]
-    outputs[1][...] = pair_grad[...]
+    for hand in (hand_result, hand_grad, hand_sums):
+        hand.wait()
+
+
+def hand_out(*refs):
+    inputs, outputs, refs = refs[:3], refs[3:15], refs[15:]
+    held, sums_flat, ready, sem = refs[:3], refs[3], refs[4:14], refs[14]
+    fetches = [
+        pltpu.make_async_copy(inputs[which], held[which], sem.at[which]) for which in range(3)
+    ]
+    hands = [
+        pltpu.make_async_copy(held[which], outputs[which], sem.at[3 + which]) for which in range(2)
+    ]
+    hands += [
+        pltpu.make_async_copy(ready[which], outputs[2 + which], sem.at[5 + which])
+        for which in range(10)
+    ]
+    for which in (2, 0, 1):
+        fetches[which].start()
+    fetches[2].wait()
+    sums_flat[...] = held[2][...].astype(F32)
     for which in range(6):
-        outputs[2 + which][0:OWNERS] = sums[pl.ds(which, OWNERS, stride=PART), :]
-        outputs[2 + which][OWNERS:] = sums[pl.ds(which + 6, OWNERS, stride=PART), :]
+        ready[which][0:OWNERS] = sums_flat[pl.ds(which, OWNERS, stride=PART), :]
+        ready[which][OWNERS:] = sums_flat[pl.ds(which + 6, OWNERS, stride=PART), :]
+        hands[2 + which].start()
     for which in range(4):
-        outputs[8 + which][...] = sums[12 + which : 13 + which]
+        ready[6 + which][...] = sums_flat[12 + which : 13 + which]
+        hands[8 + which].start()
+    for which in range(2):
+        fetches[which].wait()
+        hands[which].start()
+    for hand in hands:
+        hand.wait()
 
 
 def body(pair, cotangent, *rest):
     weights, vectors, drop_bits, tok_mask = rest[:6], rest[6:10], rest[10], rest[11]
     vmem = pltpu.VMEM
-    block, double = vmem((DEVICES * PART, 128), BF16), vmem((DEVICES * 2 * PART, 128), BF16)
-    blocks = [double] + [block] * 4 + [double] + [block] * 4
+    block = vmem((DEVICES * PART, 128), BF16)
+    blocks = [block] * 12
     squares = [vmem((SIDE, SIDE), BF16)] * 3 + [vmem((SIDE, SIDE), F32)]
-    flats = [vmem((DEVICES * 2 * PART, 128), F32)] + [vmem((DEVICES * PART, 128), F32)] * 2
+    flats = [vmem((DEVICES * PART, 128), F32)] * 2
     half, full = vmem((128, CELLS), BF16), vmem((128, CELLS), F32)
     square, tile = vmem((128, 128), BF16), (TR * TC, 128)
-    scratch = [vmem(tile, BF16)] * 2 + [square] * 6 + [vmem(tile, F32)] * 2
+    scratch = [vmem(tile, BF16)] * 2 + [square] * 6 + [vmem((1, 128), F32)] * 4
+    scratch += [vmem((TR, 128), jnp.int32), vmem((1, TOKENS), jnp.int32)]
+    scratch += [vmem(tile, F32)] * 2
     scratch += [vmem((2 * TC, 128), BF16), vmem((OWNERS * PART, 128), BF16)]
     scratch += blocks + squares + flats
     scratch += [vmem((128, 128), BF16), vmem((640, 128), BF16), vmem((128, 128), BF16)]
@@ -527,16 +560,17 @@
     scratch += [half, full, full, half, vmem((640, CELLS), BF16)]
     scratch += [vmem((4, 128, 128), F32), vmem((OWNERS * PART, 128), F32)]
     scratch += [vmem((OWNERS * PART, 128), BF16), block, vmem((PART, 128), BF16)]
-    scratch += [pltpu.SemaphoreType.DMA((8,))] * 3
+    scratch += [pltpu.SemaphoreType.DMA((8,))] * 2 + [pltpu.SemaphoreType.DMA((17,))]
+    anywhere = pl.BlockSpec(memory_space=pl.ANY)
     done = pl.pallas_call(
         kernel,
         out_shape=[
             jax.ShapeDtypeStruct(tile, BF16),
             jax.ShapeDtypeStruct(tile, BF16),
-            jax.ShapeDtypeStruct((OWNERS * PART, 128), F32),
+            jax.ShapeDtypeStruct((OWNERS * PART, 128), BF16),
         ],
-        in_specs=[pl.BlockSpec(memory_space=pl.ANY)] * 8 + [pl.BlockSpec(memory_space=vmem)] * 6,
-        out_specs=[pl.BlockSpec(memory_space=vmem)] * 3,
+        in_specs=[anywhere] * 14,
+        out_specs=[anywhere] * 3,
         scratch_shapes=scratch,
         compiler_params=pltpu.CompilerParams(
             collective_id=0, has_side_effects=True, vmem_limit_bytes=60 * 2**20
@@ -554,8 +588,13 @@
         out_shape=[jax.ShapeDtypeStruct(tile, BF16)] * 2
         + [jax.ShapeDtypeStruct((128, 128), F32)] * 6
         + [jax.ShapeDtypeStruct((1, 128), F32)] * 4,
-        in_specs=[pl.BlockSpec(memory_space=vmem)] * 3,
-        out_specs=[pl.BlockSpec(memory_space=vmem)] * 12,
+        in_specs=[anywhere] * 3,
+        out_specs=[anywhere] * 12,
+        scratch_shapes=[vmem(tile, BF16)] * 2
+        + [vmem((OWNERS * PART, 128), BF16), vmem((OWNERS * PART, 128), F32)]
+        + [vmem((128, 128), F32)] * 6
+        + [vmem((1, 128), F32)] * 4
+        + [pltpu.SemaphoreType.DMA((15,))],
         compiler_params=pltpu.CompilerParams(vmem_limit_bytes=60 * 2**20),
     )(*done)
     result, pair_grad = outs[0].reshape(TR, TC, 128), outs[1].reshape(TR, TC, 128)

time: 82.5 us -> 80.8 us (0.979)
  Pallas kernels: 81.5 us -> 79.9 us
    pallas_call x1, Pallas kernels: 79.2 us -> 77.7 us  [body(): pl.pallas_call(kernel, out_shape=[jax.ShapeDtypeStruct(tile, BF16), jax.S...]
where the time goes in v2:
time: 80.8 us; the launch traced here: 80.7 us
  Pallas kernels  79.9 us (99%)
  between operations  0.82 us (1%)
    pallas_call x1, Pallas kernels, body(): pl.pallas_call(kernel, out_shape=[jax.ShapeDtypeStruct(tile, BF16), jax.S...  77.7 us
    pallas_call x1, Pallas kernels, body(): pl.pallas_call(hand_out, out_shape=[jax.ShapeDtypeStruct(tile, BF16)] * 2...  2.18 us

profile of v2, /device:TPU:1, one launch (start us, length us, event | category | flops | bytes accessed | tf_op | source)
XLA Modules:
  0.0 80.7 jit_solution(9307163375866965447)
XLA Ops:
  0.6 77.7 %shard_map.229 = (bf16[1568,128]{1,0:T(8,128)(2,1)}, bf16[1568,128]{1,0:T(8,128)(2,1)}, bf16[1024,128]{1,0:T(8,128)(2,1)}) custom-call(bf16[1568,128]{1,0:T(8,128)(2,1)} %bitcast.13, bf16[1568,128]{1,0:T(8,128)(2,1)} %bitcast.14, bf16[128,128]{1,0:T(8,128)(2,1)} %refs_2_.1, bf16[128,128]{1,0:T(8,128)(2,1)} %refs_3_.1, bf16[128,128]{1,0:T(8,128)(2,1)} %refs_4_.1, ...), custom_call_target="tpu_custom_call" | custom-call | tf_op jit(solution)/shard_map/pallas_call | solution.py:565
  78.4 2.2 %shard_map.230 = (bf16[1568,128]{1,0:T(8,128)(2,1)}, bf16[1568,128]{1,0:T(8,128)(2,1)}, f32[128,128]{1,0:T(8,128)}, f32[128,128]{1,0:T(8,128)}, f32[128,128]{1,0...) custom-call(bf16[1568,128]{1,0:T(8,128)(2,1)} %get-tuple-element.27., ...), custom_call_target="tpu_custom_call" | custom-call | tf_op jit(solution)/shard_map/pallas_call | solution.py:586

commit v3 on v2

--- a/solution.py
+++ b/solution.py
@@ -90,6 +90,7 @@
     got_ga,
     got_gb,
     left,
+    left_t,
     right,
     turn,
     square,
@@ -114,6 +115,7 @@
     logit_keep,
     d_lifted,
     grad_mixed,
+    centered_mixed,
     mid_hat,
     mixed,
     d_all,
@@ -142,17 +144,6 @@
     def place(peer):
         return (peer // COLS, lax.rem(peer, COLS))
 
-    def greet(step, carry):
-        pl.semaphore_signal(
-            barrier,
-            inc=1,
-            device_id=place(lax.rem(me + step, DEVICES)),
-            device_id_type=pl.DeviceIdType.MESH,
-        )
-        return carry
-
-    lax.fori_loop(1, DEVICES, greet, 0)
-
     core = lax.rem(row, 2)
     at_x, at_y, at_z = lax.rem(row // 2, 2) * 2 + col // 4, row // 4, lax.rem(col, 4)
     steps_x = [lax.rem(at_x + step, 4) for step in range(4)]
@@ -163,6 +154,14 @@
 
     def device_at(x, y, z, other_core):
         return part_x[x] + part_y[y] + part_z[z] + part_core[other_core]
+
+    for offset in partners(2):
+        pl.semaphore_signal(
+            barrier,
+            inc=1,
+            device_id=place(device_at(*offset)),
+            device_id_type=pl.DeviceIdType.MESH,
+        )
 
     def send(source, target, slot, size=PART):
         mine = pl.ds(pl.multiple_of(me * size, size), size)
@@ -259,9 +258,9 @@
 
         lax.fori_loop(0, ROWS, run, 0, unroll=ROWS)
 
-    flat_a[...] = jnp.zeros_like(flat_a)
-    flat_b[...] = jnp.zeros_like(flat_b)
-    stack[256:272] = jnp.ones((16, CELLS), BF16)
+    for spare in range(HALF, PART):
+        flat_a[pl.ds(spare, 128, stride=PART), :] = jnp.zeros((128, 128), F32)
+        flat_b[pl.ds(spare, 128, stride=PART), :] = jnp.zeros((128, 128), F32)
     eye[...] = (
         lax.broadcasted_iota(jnp.int32, (128, 128), 0)
         == lax.broadcasted_iota(jnp.int32, (128, 128), 1)
@@ -273,16 +272,19 @@
     pick_cells[...] = chosen_cell.astype(BF16)
     for fetch in fetches:
         fetch.wait()
-    for place_of, weight in enumerate((w_a_proj, w_a_gate, w_b_proj, w_b_gate, w_gate)):
-        here = slice(128 * place_of, 128 * place_of + 128)
+    def put_weight(which, weight):
+        here = slice(128 * which, 128 * which + 128)
         w_in_t[here] = dot_nt(eye[...], weight[...]).astype(BF16)
         w_all[:, here] = weight[...]
-    w_out_t[...] = dot_nt(eye[...], w_out[...]).astype(BF16)
-    for place_of, vector in enumerate((in_gain, in_bias, mid_gain, mid_bias)):
+
+    def put_column(which, vector):
         column = jnp.broadcast_to(vector[...], (128, 128)).T
-        columns[place_of] = jnp.concatenate([column, column], axis=1)
-    drop_wide[...] = jnp.zeros_like(drop_wide)
-    drop_wide[0:TR] = drop[...].astype(F32)
+        columns[which] = jnp.concatenate([column, column], axis=1)
+
+    put_weight(0, w_a_proj)
+    put_weight(1, w_a_gate)
+    put_column(0, in_gain)
+    put_column(1, in_bias)
     live = jnp.sum(tok[...].astype(F32), axis=1, keepdims=True)
 
     def cell_mask(step):
@@ -321,9 +323,18 @@
     send_a[...] = flat_a[...].astype(BF16)
     pl.semaphore_wait(barrier, DEVICES - 1)
     send(send_a, got_a, 0)
+    put_weight(2, w_b_proj)
+    put_weight(3, w_b_gate)
     each(lambda step, here: front(step, here, slice(256, 512), keep_b, slope_b, flat_b))
     send_b[...] = flat_b[...].astype(BF16)
     send(send_b, got_b, 1)
+    put_weight(4, w_gate)
+    w_out_t[...] = dot_nt(eye[...], w_out[...]).astype(BF16)
+    put_column(2, mid_gain)
+    put_column(3, mid_bias)
+    stack[256:272] = jnp.ones((16, CELLS), BF16)
+    drop_wide[...] = jnp.zeros_like(drop_wide)
+    drop_wide[0:TR] = drop[...].astype(F32)
 
     def prepare(step, here):
         squash = jax.nn.sigmoid(dot(w_in_t[512:640], stack[0:128, here]))
@@ -339,15 +350,21 @@
         logit_keep[:, here] = pulled * (1.0 - squash)
         lifted_back = pulled.astype(BF16)
         d_lifted[:, here] = lifted_back
-        grad_mixed[:, here] = dot(w_out[...], lifted_back)
+        pulled_mixed = dot(w_out[...], lifted_back)
+        grad_mixed[:, here] = pulled_mixed
+        scaled = pulled_mixed * columns[2]
+        centered_mixed[:, here] = scaled - mean0(scaled)
 
     grad_cells[...] = cot[...].astype(F32)
     each(prepare)
     arrived(got_a, 0)
     assemble(got_a, left)
+    for block in range(4):
+        here = slice(128 * block, 128 * block + 128)
+        left_t[here] = dot_nt(eye[...], left[:, here]).astype(BF16)
     arrived(got_b, 1)
     assemble(got_b, right)
-    square[...] = dot_tn(left[...], right[...])
+    square[...] = dot(left_t[...], right[...])
     split(square, send_p)
     send(send_p, got_p, 2)
 
@@ -360,8 +377,8 @@
         root = lax.rsqrt(mean0(centered * centered) + LN_EPS)
         rough = centered * root
         mid_hat[:, here] = rough
-        pulled = grad_mixed[:, here] * columns[2]
-        scatter(flat_b, step, root * (pulled - mean0(pulled) - rough * mean0(pulled * rough)))
+        pulled = centered_mixed[:, here]
+        scatter(flat_b, step, root * (pulled - rough * mean0(pulled * rough)))
 
     each(tail_back)
     send_d[...] = flat_b[...].astype(BF16)
@@ -545,7 +562,7 @@
     vmem = pltpu.VMEM
     block = vmem((DEVICES * PART, 128), BF16)
     blocks = [block] * 12
-    squares = [vmem((SIDE, SIDE), BF16)] * 3 + [vmem((SIDE, SIDE), F32)]
+    squares = [vmem((SIDE, SIDE), BF16)] * 4 + [vmem((SIDE, SIDE), F32)]
     flats = [vmem((DEVICES * PART, 128), F32)] * 2
     half, full = vmem((128, CELLS), BF16), vmem((128, CELLS), F32)
     square, tile = vmem((128, 128), BF16), (TR * TC, 128)
@@ -557,7 +574,7 @@
     scratch += [vmem((128, 128), BF16), vmem((640, 128), BF16), vmem((128, 128), BF16)]
     scratch += [vmem((128, 640), BF16), vmem((4, 128, WIDE), F32), vmem((32, 128), F32)]
     scratch += [vmem((272, CELLS), BF16), full, vmem((1, CELLS), F32)] + [full] * 8
-    scratch += [half, full, full, half, vmem((640, CELLS), BF16)]
+    scratch += [half, full, full, full, half, vmem((640, CELLS), BF16)]
     scratch += [vmem((4, 128, 128), F32), vmem((OWNERS * PART, 128), F32)]
     scratch += [vmem((OWNERS * PART, 128), BF16), block, vmem((PART, 128), BF16)]
     scratch += [pltpu.SemaphoreType.DMA((8,))] * 2 + [pltpu.SemaphoreType.DMA((17,))]

time: 80.8 us -> 79.4 us (0.983)
  Pallas kernels: 79.9 us -> 78.5 us
    pallas_call x1, Pallas kernels: 77.7 us -> 76.3 us  [body(): pl.pallas_call(kernel, out_shape=[jax.ShapeDtypeStruct(tile, BF16), jax.S...]
where the time goes in v3:
time: 79.4 us; the launch traced here: 79.3 us
  Pallas kernels  78.5 us (99%)
  between operations  0.82 us (1%)
    pallas_call x1, Pallas kernels, body(): pl.pallas_call(kernel, out_shape=[jax.ShapeDtypeStruct(tile, BF16), jax.S...  76.3 us
    pallas_call x1, Pallas kernels, body(): pl.pallas_call(hand_out, out_shape=[jax.ShapeDtypeStruct(tile, BF16)] * 2...  2.18 us

profile of v3, /device:TPU:1, one launch (start us, length us, event | category | flops | bytes accessed | tf_op | source)
XLA Modules:
  0.0 79.3 jit_solution(5590973471964158273)
XLA Ops:
  0.6 76.3 %shard_map.229 = (bf16[1568,128]{1,0:T(8,128)(2,1)}, bf16[1568,128]{1,0:T(8,128)(2,1)}, bf16[1024,128]{1,0:T(8,128)(2,1)}) custom-call(bf16[1568,128]{1,0:T(8,128)(2,1)} %bitcast.13, bf16[1568,128]{1,0:T(8,128)(2,1)} %bitcast.14, bf16[128,128]{1,0:T(8,128)(2,1)} %refs_2_.1, bf16[128,128]{1,0:T(8,128)(2,1)} %refs_3_.1, bf16[128,128]{1,0:T(8,128)(2,1)} %refs_4_.1, ...), custom_call_target="tpu_custom_call" | custom-call | tf_op jit(solution)/shard_map/pallas_call | solution.py:582
  77.0 2.2 %shard_map.230 = (bf16[1568,128]{1,0:T(8,128)(2,1)}, bf16[1568,128]{1,0:T(8,128)(2,1)}, f32[128,128]{1,0:T(8,128)}, f32[128,128]{1,0:T(8,128)}, f32[128,128]{1,0...) custom-call(bf16[1568,128]{1,0:T(8,128)(2,1)} %get-tuple-element.27., ...), custom_call_target="tpu_custom_call" | custom-call | tf_op jit(solution)/shard_map/pallas_call | solution.py:603

commit v4 on v3

--- a/solution.py
+++ b/solution.py
@@ -17,7 +17,9 @@
 SIDE = 512
 PART = 16
 HALF = 14
+BLOCK = DEVICES * PART
 OWNERS = DEVICES // 2
+SHARES = OWNERS * PART
 BF16 = jnp.bfloat16
 F32 = jnp.float32
 
@@ -320,13 +322,13 @@
 
     result_cells[...] = pair[...].astype(F32)
     each(front_a)
-    send_a[...] = flat_a[...].astype(BF16)
+    send_a[...] = flat_a[0:BLOCK].astype(BF16)
     pl.semaphore_wait(barrier, DEVICES - 1)
     send(send_a, got_a, 0)
     put_weight(2, w_b_proj)
     put_weight(3, w_b_gate)
     each(lambda step, here: front(step, here, slice(256, 512), keep_b, slope_b, flat_b))
-    send_b[...] = flat_b[...].astype(BF16)
+    send_b[...] = flat_b[0:BLOCK].astype(BF16)
     send(send_b, got_b, 1)
     put_weight(4, w_gate)
     w_out_t[...] = dot_nt(eye[...], w_out[...]).astype(BF16)
@@ -369,7 +371,7 @@
     send(send_p, got_p, 2)
 
     arrived(got_p, 2)
-    flat_a[...] = got_p[...].astype(F32)
+    flat_a[0:BLOCK] = got_p[...].astype(F32)
 
     def tail_back(step, here):
         cells = gather(flat_a, step)
@@ -381,7 +383,7 @@
         scatter(flat_b, step, root * (pulled - rough * mean0(pulled * rough)))
 
     each(tail_back)
-    send_d[...] = flat_b[...].astype(BF16)
+    send_d[...] = flat_b[0:BLOCK].astype(BF16)
     send(send_d, got_d, 3)
 
     totals[...] = jnp.zeros_like(totals)
@@ -446,16 +448,16 @@
         return run
 
     arrived(got_ga, 4)
-    flat_a[...] = got_ga[...].astype(F32)
+    flat_a[0:BLOCK] = got_ga[...].astype(F32)
     each(front_back(0, flat_a, keep_a, slope_a))
     put_front(0, 2)
     arrived(got_gb, 5)
-    flat_b[...] = got_gb[...].astype(F32)
+    flat_b[0:BLOCK] = got_gb[...].astype(F32)
     each(front_back(256, flat_b, keep_b, slope_b))
     put_front(2, 4)
     put_vector(0)
     put_vector(1)
-    sums_send[...] = sums_flat[...].astype(BF16)
+    sums_send[...] = sums_flat[0:SHARES].astype(BF16)
 
     chip = (row // 2) * COLS + col
     mine = pl.ds(pl.multiple_of(me * PART, PART), PART)
@@ -542,7 +544,7 @@
     for which in (2, 0, 1):
         fetches[which].start()
     fetches[2].wait()
-    sums_flat[...] = held[2][...].astype(F32)
+    sums_flat[0:SHARES] = held[2][...].astype(F32)
     for which in range(6):
         ready[which][0:OWNERS] = sums_flat[pl.ds(which, OWNERS, stride=PART), :]
         ready[which][OWNERS:] = sums_flat[pl.ds(which + 6, OWNERS, stride=PART), :]
@@ -563,7 +565,7 @@
     block = vmem((DEVICES * PART, 128), BF16)
     blocks = [block] * 12
     squares = [vmem((SIDE, SIDE), BF16)] * 4 + [vmem((SIDE, SIDE), F32)]
-    flats = [vmem((DEVICES * PART, 128), F32)] * 2
+    flats = [vmem((BLOCK + PART, 128), F32)] * 2
     half, full = vmem((128, CELLS), BF16), vmem((128, CELLS), F32)
     square, tile = vmem((128, 128), BF16), (TR * TC, 128)
     scratch = [vmem(tile, BF16)] * 2 + [square] * 6 + [vmem((1, 128), F32)] * 4
@@ -575,7 +577,7 @@
     scratch += [vmem((128, 640), BF16), vmem((4, 128, WIDE), F32), vmem((32, 128), F32)]
     scratch += [vmem((272, CELLS), BF16), full, vmem((1, CELLS), F32)] + [full] * 8
     scratch += [half, full, full, full, half, vmem((640, CELLS), BF16)]
-    scratch += [vmem((4, 128, 128), F32), vmem((OWNERS * PART, 128), F32)]
+    scratch += [vmem((4, 128, 128), F32), vmem((SHARES + PART, 128), F32)]
     scratch += [vmem((OWNERS * PART, 128), BF16), block, vmem((PART, 128), BF16)]
     scratch += [pltpu.SemaphoreType.DMA((8,))] * 2 + [pltpu.SemaphoreType.DMA((17,))]
     anywhere = pl.BlockSpec(memory_space=pl.ANY)
@@ -608,7 +610,7 @@
         in_specs=[anywhere] * 3,
         out_specs=[anywhere] * 12,
         scratch_shapes=[vmem(tile, BF16)] * 2
-        + [vmem((OWNERS * PART, 128), BF16), vmem((OWNERS * PART, 128), F32)]
+        + [vmem((SHARES, 128), BF16), vmem((SHARES + PART, 128), F32)]
         + [vmem((128, 128), F32)] * 6
         + [vmem((1, 128), F32)] * 4
         + [pltpu.SemaphoreType.DMA((15,))],

time: 79.4 us -> 79.5 us (level)
  no operation moved by 1% of the time
where the time goes in v4:
time: 79.5 us; the launch traced here: 79.4 us
  Pallas kernels  78.6 us (99%)
  between operations  0.82 us (1%)
    pallas_call x1, Pallas kernels, body(): pl.pallas_call(kernel, out_shape=[jax.ShapeDtypeStruct(tile, BF16), jax.S...  76.4 us
    pallas_call x1, Pallas kernels, body(): pl.pallas_call(hand_out, out_shape=[jax.ShapeDtypeStruct(tile, BF16)] * 2...  2.18 us

profile of v4, /device:TPU:1, one launch (start us, length us, event | category | flops | bytes accessed | tf_op | source)
XLA Modules:
  0.0 79.4 jit_solution(8892663808808983680)
XLA Ops:
  0.6 76.4 %shard_map.229 = (bf16[1568,128]{1,0:T(8,128)(2,1)}, bf16[1568,128]{1,0:T(8,128)(2,1)}, bf16[1024,128]{1,0:T(8,128)(2,1)}) custom-call(bf16[1568,128]{1,0:T(8,128)(2,1)} %bitcast.13, bf16[1568,128]{1,0:T(8,128)(2,1)} %bitcast.14, bf16[128,128]{1,0:T(8,128)(2,1)} %refs_2_.1, bf16[128,128]{1,0:T(8,128)(2,1)} %refs_3_.1, bf16[128,128]{1,0:T(8,128)(2,1)} %refs_4_.1, ...), custom_call_target="tpu_custom_call" | custom-call | tf_op jit(solution)/shard_map/pallas_call | solution.py:584
  77.0 2.2 %shard_map.230 = (bf16[1568,128]{1,0:T(8,128)(2,1)}, bf16[1568,128]{1,0:T(8,128)(2,1)}, f32[128,128]{1,0:T(8,128)}, f32[128,128]{1,0:T(8,128)}, f32[128,128]{1,0...) custom-call(bf16[1568,128]{1,0:T(8,128)(2,1)} %get-tuple-element.27., ...), custom_call_target="tpu_custom_call" | custom-call | tf_op jit(solution)/shard_map/pallas_call | solution.py:605

commit v5 on v4

--- a/solution.py
+++ b/solution.py
@@ -143,25 +143,23 @@
     me = row * COLS + col
     barrier = pltpu.get_barrier_semaphore()
 
-    def place(peer):
-        return (peer // COLS, lax.rem(peer, COLS))
-
     core = lax.rem(row, 2)
     at_x, at_y, at_z = lax.rem(row // 2, 2) * 2 + col // 4, row // 4, lax.rem(col, 4)
     steps_x = [lax.rem(at_x + step, 4) for step in range(4)]
-    part_x = [(step // 2) * 16 + lax.rem(step, 2) * 4 for step in steps_x]
-    part_y = [lax.rem(at_y + step, 4) * 32 for step in range(4)]
-    part_z = [lax.rem(at_z + step, 4) for step in range(4)]
-    part_core = [lax.rem(core + step, 2) * 8 for step in range(2)]
+    row_x = [(step // 2) * 2 for step in steps_x]
+    row_y = [lax.rem(at_y + step, 4) * 4 for step in range(4)]
+    row_core = [core, 1 - core]
+    col_x = [lax.rem(step, 2) * 4 for step in steps_x]
+    col_z = [lax.rem(at_z + step, 4) for step in range(4)]
 
     def device_at(x, y, z, other_core):
-        return part_x[x] + part_y[y] + part_z[z] + part_core[other_core]
+        return row_y[y] + row_x[x] + row_core[other_core], col_x[x] + col_z[z]
 
     for offset in partners(2):
         pl.semaphore_signal(
             barrier,
             inc=1,
-            device_id=place(device_at(*offset)),
+            device_id=device_at(*offset),
             device_id_type=pl.DeviceIdType.MESH,
         )
 
@@ -169,13 +167,14 @@
         mine = pl.ds(pl.multiple_of(me * size, size), size)
 
         for offset in partners(2):
-            peer = device_at(*offset)
+            there = device_at(*offset)
+            peer = there[0] * COLS + there[1]
             pltpu.make_async_remote_copy(
                 src_ref=source.at[pl.ds(pl.multiple_of(peer * size, size), size)],
                 dst_ref=target.at[mine],
                 send_sem=send_sem.at[slot],
                 recv_sem=recv_sem.at[slot],
-                device_id=place(peer),
+                device_id=there,
                 device_id_type=pl.DeviceIdType.MESH,
             ).start()
         target[mine] = source[mine]
@@ -464,14 +463,14 @@
     owned = pl.ds(pl.multiple_of(chip * PART, PART), PART)
 
     def start_sum(x, y, z):
-        home = part_x[x] + part_y[y] + part_z[z]
-        owner = (home // 16) * COLS + lax.rem(home, COLS)
+        there = row_y[y] + row_x[x], col_x[x] + col_z[z]
+        owner = there[0] * (COLS // 2) + there[1]
         pltpu.make_async_remote_copy(
             src_ref=sums_send.at[pl.ds(pl.multiple_of(owner * PART, PART), PART)],
             dst_ref=sums_got.at[mine],
             send_sem=send_sem.at[6],
             recv_sem=recv_sem.at[6],
-            device_id=place(home),
+            device_id=there,
             device_id_type=pl.DeviceIdType.MESH,
         ).start()
 
@@ -506,7 +505,7 @@
                 dst_ref=sums.at[owned],
                 send_sem=send_sem.at[7],
                 recv_sem=recv_sem.at[7],
-                device_id=place(device_at(*offset)),
+                device_id=device_at(*offset),
                 device_id_type=pl.DeviceIdType.MESH,
             ).start()
 

time: 79.5 us -> 79.2 us (level)
  no operation moved by 1% of the time
where the time goes in v5:
time: 79.2 us; the launch traced here: 79.1 us
  Pallas kernels  78.3 us (99%)
  between operations  0.82 us (1%)
    pallas_call x1, Pallas kernels, body(): pl.pallas_call(kernel, out_shape=[jax.ShapeDtypeStruct(tile, BF16), jax.S...  76.1 us
    pallas_call x1, Pallas kernels, body(): pl.pallas_call(hand_out, out_shape=[jax.ShapeDtypeStruct(tile, BF16)] * 2...  2.18 us

profile of v5, /device:TPU:1, one launch (start us, length us, event | category | flops | bytes accessed | tf_op | source)
XLA Modules:
  0.0 79.1 jit_solution(3175383934086201161)
XLA Ops:
  0.6 76.1 %shard_map.229 = (bf16[1568,128]{1,0:T(8,128)(2,1)}, bf16[1568,128]{1,0:T(8,128)(2,1)}, bf16[1024,128]{1,0:T(8,128)(2,1)}) custom-call(bf16[1568,128]{1,0:T(8,128)(2,1)} %bitcast.13, bf16[1568,128]{1,0:T(8,128)(2,1)} %bitcast.14, bf16[128,128]{1,0:T(8,128)(2,1)} %refs_2_.1, bf16[128,128]{1,0:T(8,128)(2,1)} %refs_3_.1, bf16[128,128]{1,0:T(8,128)(2,1)} %refs_4_.1, ...), custom_call_target="tpu_custom_call" | custom-call | tf_op jit(solution)/shard_map/pallas_call | solution.py:583
  76.7 2.2 %shard_map.230 = (bf16[1568,128]{1,0:T(8,128)(2,1)}, bf16[1568,128]{1,0:T(8,128)(2,1)}, f32[128,128]{1,0:T(8,128)}, f32[128,128]{1,0:T(8,128)}, f32[128,128]{1,0...) custom-call(bf16[1568,128]{1,0:T(8,128)(2,1)} %get-tuple-element.27., ...), custom_call_target="tpu_custom_call" | custom-call | tf_op jit(solution)/shard_map/pallas_call | solution.py:604
